TPU v7x, 32 devices: a whole 2x2x4 slice. The times are simulated.
32 devices in a mesh: blk: 16 (over z, y, core), narrow: 2 (over x).
Axes of the slice: x: 2, y: 2, z: 4, core: 2. Of those that a mesh axis runs over, the one named last changes fastest.
Arguments:
- vectors: bfloat16 [8192, 768], P(('blk', 'narrow')), may hold values from -8 to 8
- centroids: bfloat16 [65536, 768], P('blk'), may hold values from -1 to 1
- list_owner: int32 [8192, 1], P(('blk', 'narrow')), may hold values from 0 to 15; in each aligned block of 256 rows (0 to 255, 256 to 511, ...) at most 32 rows name the same one
- list_local: int32 [8192], P(('blk', 'narrow')), may hold values from 0 to 4095
Outputs:
- panel_sums: float32 [65536, 768], P(('blk', 'narrow'))
- panel_counts: float32 [65536], P(('blk', 'narrow'))
- posted: bfloat16 [16384, 768], P(('blk', 'narrow'))
Inputs may be any that keep to these rules, and one draw needn't show every extreme that they name: `list_owner`: among the 256 rows of one device, at most 32 name the same owner, and in every draw some device's rows name some owner exactly 32 times.
All inputs are finite; a program needn't handle non-finite values.
Results may differ from a plain program's by a relative error of at most 0.0065.
Values may be sent and summed in bfloat16 or wider, within the bound.
A program may use at most 128 MiB of HBM per device.

v0:
```python
import jax
import jax.numpy as jnp
from jax import lax
from jax.sharding import PartitionSpec as P

temper = 0.5


def passed_along(x, axis, by):
    peers = lax.axis_size(axis)
    return lax.ppermute(x, axis, [(i, (i + by) % peers) for i in range(peers)])


def for_sending(x):
    return jax.tree.map(lambda a: a.astype(jnp.bfloat16) if a.dtype == jnp.float32 else a, x)


def window_logits(row_block, panel_rows):
    norms = jnp.sum(jnp.square(panel_rows.astype(jnp.float32)), axis=1)
    product = lax.dot_general(
        row_block, panel_rows, (((1,), (1,)), ((), ())), preferred_element_type=jnp.float32
    )
    return (product - 0.5 * norms[None, :]) / temper


def post_rows(residual, owner, local, owner_count, capacity, panel_size):
    row_total = residual.shape[0]
    places = jnp.arange(row_total, dtype=jnp.int32)
    sort_key = (owner * panel_size + local) * row_total + places
    order = jnp.argsort(sort_key)
    sorted_owner = owner[order]
    owner_ids = jnp.arange(owner_count, dtype=jnp.int32)
    onehot = (owner[:, None] == owner_ids[None, :]).astype(jnp.int32)
    owner_rows = jnp.sum(onehot, axis=0)
    owner_start = jnp.cumsum(owner_rows) - owner_rows
    first_place = jnp.sum(
        jnp.where(sorted_owner[:, None] == owner_ids[None, :], owner_start[None, :], 0), axis=1
    )
    slot_index = places - first_place
    buffer = jnp.zeros((owner_count, capacity, residual.shape[1]), residual.dtype)
    return buffer.at[sorted_owner, slot_index].set(residual[order])


def weighted_terms(weights, row_block):
    summed = lax.dot_general(
        weights, row_block, (((0,), (0,)), ((), ())), preferred_element_type=jnp.float32
    )
    tally = jnp.sum(weights.astype(jnp.float32), axis=0)
    return (summed.astype(jnp.bfloat16), tally.astype(jnp.bfloat16))


def body(vectors, centroids, list_owner, list_local):
    owner_count = lax.axis_size("blk")
    vec_rows = vectors.shape[0]
    capacity = max(2, 2 * vec_rows // owner_count)
    panels = [centroids]
    panels.append(passed_along(panels[-1], "blk", 1))
    logit_list = [window_logits(vectors, panel_rows) for panel_rows in panels]
    row_top = jnp.max(jnp.stack([jnp.max(logits, axis=1) for logits in logit_list]), axis=0)
    row_total = sum((jnp.sum(jnp.exp(logits - row_top[:, None]), axis=1) for logits in logit_list))
    log_total = row_top + jnp.log(row_total)
    weight_list = [
        jnp.exp(logits - log_total[:, None]).astype(jnp.bfloat16) for logits in logit_list
    ]
    mixture = sum(
        (
            jnp.dot(weights, panel_rows, preferred_element_type=jnp.float32)
            for weights, panel_rows in zip(weight_list, panels)
        )
    )
    term_list = [weighted_terms(weights, vectors) for weights in weight_list]
    home_terms = [term_list[0]]
    home_terms.append(passed_along(for_sending(term_list[1]), "blk", -1))
    summed = (
        lax.psum_scatter(
            jnp.stack([pair[0] for pair in home_terms]), "narrow", scatter_dimension=1, tiled=True
        ).astype(jnp.float32),
        lax.psum_scatter(
            jnp.stack([pair[1] for pair in home_terms]), "narrow", scatter_dimension=1, tiled=True
        ).astype(jnp.float32),
    )
    panel_sums = jnp.sum(summed[0], axis=0)
    panel_counts = jnp.sum(summed[1], axis=0)
    residual = (vectors.astype(jnp.float32) - mixture).astype(jnp.bfloat16)
    buffer = post_rows(
        residual, list_owner[:, 0], list_local, owner_count, capacity, centroids.shape[0]
    )
    received = lax.all_to_all(buffer, "blk", split_axis=0, concat_axis=0, tiled=True)
    posted = received.reshape(owner_count * capacity, vectors.shape[1])
    return (panel_sums, panel_counts, posted)


def solution(mesh):
    in_specs = (
        P(("blk", "narrow"), None),
        P("blk", None),
        P(("blk", "narrow"), None),
        P(("blk", "narrow")),
    )
    out_specs = (P(("blk", "narrow"), None), P(("blk", "narrow")), P(("blk", "narrow"), None))
    return jax.shard_map(body, mesh=mesh, in_specs=in_specs, out_specs=out_specs, check_vma=False)
```

profile of v0, /device:TPU:13, one launch (start us, length us, event | category | flops | bytes accessed | tf_op | source)
XLA Modules:
  0.0 344.9 jit_solution(8669579726439208381)
XLA Ops:
  7.2 0.0 reduce-scatter.7.cloned.1.call-start
  7.2 0.0 copy-start.2
  7.2 1.9 collective-permute-start
  9.1 4.1 %multiply_reduce_fusion.1 = f32[4096]{0:T(1024)S(1)} fusion(bf16[4096,768]{1,0:T(8,128)(2,1)} %param.5), kind=kLoop, calls=%fused_computation.6 | loop fusion | flops 9433088 | bytes 6307840 | tf_op jit(solution)/shard_map/reduce_sum | solution.py:19
  13.2 0.0 copy-done.2
  13.2 2.9 fusion.8
  16.1 0.0 copy-start.4
  16.2 61.2 %collective-permute-done = bf16[4096,768]{1,0:T(8,128)(2,1)S(1)} collective-permute-done((bf16[4096,768]{1,0:T(8,128)(2,1)}, bf16[4096,768]{1,0:T(8,128)(2,1)S(1)}, u32[]{:S(2)}, u32[]{:S(2)}) %collective-permute-start) | collective-permute-done | bytes 6291488 | tf_op jit(solution)/shard_map/ppermute | solution.py:11
  77.3 0.0 copy-start.3
  77.3 1.3 multiply_reduce_fusion
  78.6 0.0 copy-done.4
  78.6 1.9 fusion.9
  80.6 0.0 copy-done.3
  80.6 1.3 exponential_reduce_fusion
  81.9 1.4 fusion.6
  83.3 0.0 copy-start.1
  83.3 4.6 %convolution_convert_fusion = bf16[4096,768]{1,0:T(8,128)(2,1)} fusion(bf16[256,4096]{1,0:T(8,128)(2,1)S(1)} %get-tuple-element.12, bf16[256,768]{1,0:T(8,128)(2,1)S(1)} %copy-done.4), kind=kOutput, calls=%fused_computation.7 | convolution fusion | flops 1613758464 | bytes 8781824 | tf_op jit(solution)/shard_map/dot_general | solution.py:45
  87.9 1.2 collective-permute-start.1
  89.1 0.0 collective-permute-start.2
  89.1 0.0 copy-done.1
  89.1 4.6 %fusion = bf16[1,4096,768]{2,1,0:T(8,128)(2,1)} fusion(bf16[256,4096]{1,0:T(8,128)(2,1)S(1)} %get-tuple-element.8, bf16[256,768]{1,0:T(8,128)(2,1)S(1)} %copy-done.4), kind=kOutput, calls=%fused_computation.9 | convolution fusion | flops 1613758464 | bytes 8781824 | tf_op jit(solution)/shard_map/dot_general | solution.py:45
  93.7 66.4 %collective-permute-done.2 = bf16[4096]{0:T(1024)(128)(2,1)S(1)} collective-permute-done((bf16[4096]{0:T(1024)(128)(2,1)S(1)}, bf16[4096]{0:T(1024)(128)(2,1)S(1)}, u32[]{:S(2)}, u32[]{:S(2)}) %collective-permute-start.2) | collective-permute-done | bytes 8224 | tf_op jit(solution)/shard_map/ppermute | solution.py:11
  160.2 1.4 copy.11
  161.6 0.0 reduce-scatter.7.cloned.1.call-update
  161.6 0.0 reduce-scatter.5.cloned.1.call-start
  161.7 0.0 collective-permute-done.1
  161.7 10.9 %pad_maximum_fusion = bf16[2,4096,768]{2,1,0:T(8,128)(2,1)} fusion(bf16[1,4096,768]{2,1,0:T(8,128)(2,1)} %bitcast.1, bf16[1,4096,768]{2,1,0:T(8,128)(2,1)} %fusion), kind=kLoop, calls=%fused_computation.3 | loop fusion | flops 6291456 | bytes 25165824 | tf_op jit(solution)/shard_map/stack | solution.py:76
  172.6 0.0 copy-start
  172.6 0.0 copy-start.5
  172.6 0.0 reduce-scatter.5.cloned.1.call-update
  172.6 0.7 copy-done
  173.3 0.0 copy-done.5
  173.3 3.2 sort.17
  176.5 1.9 gather_fusion
  178.4 0.1 convert_reduce_fusion.1
  178.5 0.1 copy.10
  178.7 0.1 reduce.4
  178.8 0.1 select_reduce_fusion
  178.9 5.2 %fusion.10 = f32[256,768]{1,0:T(8,128)S(1)} fusion(bf16[256,4096]{1,0:T(8,128)(2,1)} %copy-done.1, bf16[4096,768]{1,0:T(8,128)(2,1)} %param.5), kind=kOutput, calls=%fused_computation.43 | convolution fusion | flops 1610612736 | bytes 9175040 | tf_op jit(solution)/shard_map/dot_general | solution.py:67
  184.2 4.6 %fusion.4 = bf16[256,768]{1,0:T(8,128)(2,1)S(1)} fusion(f32[256,768]{1,0:T(8,128)S(1)} %fusion.10, bf16[256,4096]{1,0:T(8,128)(2,1)S(1)} %get-tuple-element.12, bf16[4096,768]{1,0:T(8,128)(2,1)} %copy-done.3, bf16[256,768]{1,0:T(8,128)(2,1)S(1)} %copy-done.4), kind=kOutput, calls=%fused_computation.20 | convolution fusion | flops 1611399168 | bytes 9961472 | tf_op jit(solution)/shard_map/dot_general | solution.py:67
  188.7 1.2 gather_fusion.1
  189.9 1.0 broadcast_in_dim.12
  190.9 37.4 %scatter_fusion = bf16[16,32,768]{2,1,0:T(8,128)(2,1)} fusion(bf16[16,32,768]{2,1,0:T(8,128)(2,1)} %broadcast_in_dim.12, s32[256]{0:T(256)S(1)} %bitcast.27, bf16[256,768]{1,0:T(8,128)(2,1)S(1)} %gather_fusion.1), kind=kCustom, calls=%fused_computation.2 | custom fusion | bytes 1181696 | tf_op jit(solution)/shard_map/scatter | solution.py:41
  228.3 5.7 %all-to-all-start = ((bf16[16,32,768]{2,1,0:T(8,128)(2,1)}), bf16[16,32,768]{2,1,0:T(8,128)(2,1)S(1)}, u32[]{:S(2)}, u32[]{:S(2)}) async-start(bf16[16,32,768]{2,1,0:T(8,128)(2,1)} %scatter_fusion), calls=%async_computation.1 | async-start | bytes 1572864 | tf_op jit(solution)/shard_map/all_to_all | solution.py:88
  234.0 0.0 reduce-scatter.7.cloned.1.call-done
  234.0 1.3 copy.12
  235.3 0.6 convert_reduce_fusion.2
  235.9 17.7 %all-to-all-done = bf16[16,32,768]{2,1,0:T(8,128)(2,1)S(1)} async-done(((bf16[16,32,768]{2,1,0:T(8,128)(2,1)}), bf16[16,32,768]{2,1,0:T(8,128)(2,1)S(1)}, u32[]{:S(2)}, u32[]{:S(2)}) %all-to-all-start) | async-done | bytes 786464 | tf_op jit(solution)/shard_map/all_to_all | solution.py:88
  253.7 76.4 %reduce-scatter.5.cloned.1.call-done = bf16[2,2048,768]{2,1,0:T(8,128)(2,1)} async-done(((bf16[2,4096,768]{2,1,0:T(8,128)(2,1)}), bf16[2,2048,768]{2,1,0:T(8,128)(2,1)}) %reduce-scatter.5.cloned.1.call-update) | async-done | bytes 6291472 | tf_op jit(solution)/shard_map/reduce_scatter | solution.py:75
  330.0 7.1 %convert_reduce_fusion = f32[2048,768]{1,0:T(8,128)} fusion(bf16[2,2048,768]{2,1,0:T(8,128)(2,1)} %reduce-scatter.5.cloned.1.call-done), kind=kLoop, calls=%fused_computation.4 | loop fusion | flops 4718592 | bytes 12582912 | tf_op jit(solution)/shard_map/reduce_sum | solution.py:82
  337.1 0.9 copy.15
  (14 shorter events, 0.2 us)
Async XLA Ops:
  7.2 226.9 %reduce-scatter.7.cloned.1.call-start = ((), (), s32[]{:S(2)}) async-start(), calls=%async_computation.4 | async-start | bytes 1572864
  7.2 6.0 %copy-start.2 = (bf16[4096,768]{1,0:T(8,128)(2,1)S(1)}, bf16[4096,768]{1,0:T(8,128)(2,1)}, u32[]{:S(2)}) copy-start(bf16[4096,768]{1,0:T(8,128)(2,1)} %param.5) | copy-start | bytes 18874372
  7.2 70.1 %collective-permute-start = (bf16[4096,768]{1,0:T(8,128)(2,1)}, bf16[4096,768]{1,0:T(8,128)(2,1)S(1)}, u32[]{:S(2)}, u32[]{:S(2)}) collective-permute-start(bf16[4096,768]{1,0:T(8,128)(2,1)} %param.5), channel_id=1, source_target_pairs={{0,2},{2,4},{4,6},{6,8},{8,10},{10,12},{12,14},{14,16},{16,18},{18... | collective-permute-start | bytes 18874376 | tf_op jit(solution)/shard_map/ppermute | solution.py:11
  16.1 62.5 %copy-start.4 = (bf16[256,768]{1,0:T(8,128)(2,1)S(1)}, bf16[256,768]{1,0:T(8,128)(2,1)}, u32[]{:S(2)}) copy-start(bf16[256,768]{1,0:T(8,128)(2,1)} %param.4) | copy-start | bytes 1179652
  77.3 3.3 copy-start.3
  83.3 5.8 %copy-start.1 = (bf16[256,4096]{1,0:T(8,128)(2,1)}, bf16[256,4096]{1,0:T(8,128)(2,1)S(1)}, u32[]{:S(2)}) copy-start(bf16[256,4096]{1,0:T(8,128)(2,1)S(1)} %get-tuple-element.8) | copy-start | bytes 6291460
  87.9 73.8 %collective-permute-start.1 = (bf16[4096,768]{1,0:T(8,128)(2,1)}, bf16[4096,768]{1,0:T(8,128)(2,1)}, u32[]{:S(2)}, u32[]{:S(2)}) collective-permute-start(bf16[4096,768]{1,0:T(8,128)(2,1)} %convolution_convert_fusion), channel_id=1, source_target_pairs={{0,30},{2,0},{4,2},{6,4},{8,6},{10,8},{12,10},{14,12},{16,14},{18,... | collective-permute-start | bytes 18874376 | tf_op jit(solution)/shard_map/ppermute | solution.py:11
  89.1 71.0 %collective-permute-start.2 = (bf16[4096]{0:T(1024)(128)(2,1)S(1)}, bf16[4096]{0:T(1024)(128)(2,1)S(1)}, u32[]{:S(2)}, u32[]{:S(2)}) collective-permute-start(bf16[4096]{0:T(1024)(128)(2,1)S(1)} %get-tuple-element.11), channel_id=1, source_target_pairs={{0,30},{2,0},{4,2},{6,4},{8,6},{10,8},{12,10},{14,12},{16,14},{18,... | collective-permute-start | bytes 24584 | tf_op jit(solution)/shard_map/ppermute | solution.py:11
  161.6 168.4 %reduce-scatter.5.cloned.1.call-start = ((), (), s32[]{:S(2)}) async-start(), calls=%async_computation.3 | async-start | bytes 18874368 | tf_op jit(solution)/shard_map/reduce_scatter | solution.py:75
  172.6 0.7 copy-start
  172.6 0.7 copy-start.5
  228.3 25.3 %all-to-all-start = ((bf16[16,32,768]{2,1,0:T(8,128)(2,1)}), bf16[16,32,768]{2,1,0:T(8,128)(2,1)S(1)}, u32[]{:S(2)}, u32[]{:S(2)}) async-start(bf16[16,32,768]{2,1,0:T(8,128)(2,1)} %scatter_fusion), calls=%async_computation.1 | async-start | bytes 1572864 | tf_op jit(solution)/shard_map/all_to_all | solution.py:88
Sparse Core Ops, SparseCore 0:
  161.8 21.3 reduce-scatter.6
  185.6 144.4 reduce-scatter.4
where the time goes:
time: 348 us; the launch traced here: 345 us
  waiting for transfers between devices  222 us (64%)
  local copies, waits for them, and re-layouts  45.9 us (13%)
  other arithmetic  30.4 us (9%)
  matrix products  23.9 us (7%)
  between operations  14.2 us (4%)
  starting transfers between devices  8.88 us (3%)
    ppermute x3, waiting for transfers between devices, passed_along(): return lax.ppermute(x, axis, [(i, (i + by) % peers) for i in range(peers)])  128 us
    reduce_scatter x1, waiting for transfers between devices, body(): lax.psum_scatter(jnp.stack([pair[0] for pair in home_terms]), 'narrow', s...  76.4 us
    scatter x1, local copies, waits for them, and re-layouts, post_rows(): return buffer.at[sorted_owner, slot_index].set(residual[order])  37.4 us
    all_to_all x1, waiting for transfers between devices, body(): lax.all_to_all(buffer, 'blk', split_axis=0, concat_axis=0, tiled=True)  17.7 us
    another operation x1, other arithmetic, body(): jnp.stack([pair[0] for pair in home_terms])  10.9 us
    dot_general x2, matrix products, body(): jnp.dot(weights, panel_rows, preferred_element_type=jnp.float32)  9.83 us
    dot_general x2, matrix products, weighted_terms(): lax.dot_general(weights, row_block, (((0,), (0,)), ((), ())), preferred_e...  9.16 us
    reduce_sum x1, other arithmetic, body(): panel_sums = jnp.sum(summed[0], axis=0)  7.1 us
  transfers between devices with their start and end apart: 6, of which 4 were waited for; matrix products, arithmetic and copies ran while one was open for 23% of the time, Pallas kernels for 0%

commit v1 on v0

v1 whole, which is shorter than its diff:
```python
import functools

import jax
import jax.numpy as jnp
from jax import lax
from jax.experimental import pallas as pl
from jax.experimental.pallas import tpu as pltpu
from jax.sharding import PartitionSpec as P

MESH = pl.DeviceIdType.MESH
F32 = jnp.float32
BF16 = jnp.bfloat16
EARLY = 2


def kernel(
    nb, nn, cap,
    vec_ref, cen_ref, owner_ref, local_ref,
    sums_ref, counts_ref, posted_ref,
    v_all, cen, cen_t, vec_t, norms, logit, prob, stats, mine, parts, got, total, place, box, acc,
    local_sem, v_send, v_recv, s_send, s_recv, m_send, m_recv, a_send, a_recv, o_sem,
):
    b = lax.axis_index("blk")
    n = lax.axis_index("narrow")
    before, after = lax.rem(b + nb - 1, nb), lax.rem(b + 1, nb)
    rows, width = vec_ref.shape
    cents = cen.shape[0]
    tile = min(512, cents)
    tiles = cents // tile

    def remote(src, dst, send, recv, blk, narrow):
        return pltpu.make_async_remote_copy(
            src_ref=src, dst_ref=dst, send_sem=send, recv_sem=recv,
            device_id={"blk": blk, "narrow": narrow}, device_id_type=MESH,
        )

    own_rows = pltpu.make_async_copy(vec_ref, v_all.at[n], local_sem.at[0])
    own_rows.start()
    own_cents = pltpu.make_async_copy(
        cen_ref.at[pl.ds(pl.multiple_of(n * cents, 16), cents)], cen, local_sem.at[1]
    )
    own_cents.start()

    barrier = pltpu.get_barrier_semaphore()

    def greet(blk, narrow):
        pl.semaphore_signal(
            barrier, inc=1, device_id={"blk": blk, "narrow": narrow}, device_id_type=MESH
        )

    for j in range(1, nn):
        other = lax.rem(n + j, nn)
        for blk in (b, before, after):
            greet(blk, other)

    @pl.loop(1, nb)
    def _(i):
        greet(lax.rem(b + i, nb), n)

    pl.semaphore_wait(barrier, 3 * (nn - 1) + nb - 1)

    def v_copy(j, back):
        other = lax.rem(n + j, nn)
        slot = n + nn * back
        at = j + nn * back
        return remote(
            vec_ref, v_all.at[slot], v_send.at[at], v_recv.at[slot], before if back else b, other
        )

    for j in range(nn):
        v_copy(j, 1).start()
        if j:
            v_copy(j, 0).start()

    own_cents.wait()
    for t in range(tiles):
        at = pl.ds(t * tile, tile)
        block = cen[at, :]
        wide = block.astype(F32)
        norms[at, :] = jnp.sum(wide * wide, axis=1, keepdims=True)
        cen_t[:, at] = block.T
    own_rows.wait()
    vec_t[...] = v_all[n].T

    up = lax.broadcasted_iota(jnp.int32, (rows, rows), 0)
    across = lax.broadcasted_iota(jnp.int32, (rows, rows), 1)
    owner_col = owner_ref[...].astype(F32)
    local_row = local_ref[...].astype(F32)
    owner_row = jnp.sum(jnp.where(up == across, owner_col, 0.0), axis=0, keepdims=True)
    local_col = jnp.sum(jnp.where(up == across, local_row, 0.0), axis=1, keepdims=True)
    ahead = (local_col < local_row) | ((local_col == local_row) & (up < across))
    rank = jnp.sum(
        jnp.where((owner_col == owner_row) & ahead, 1.0, 0.0), axis=0, keepdims=True
    )
    goes_to = owner_row * float(cap) + rank
    slots = lax.broadcasted_iota(jnp.int32, (nb * cap, rows), 0).astype(F32)
    place[...] = jnp.where(slots == goes_to, 1.0, 0.0).astype(BF16)

    def attend(step):
        far = step // nn
        k = lax.rem(n + step, nn)
        slot = k + nn * far
        vecs = v_all[slot]
        top = None
        for t in range(tiles):
            at = pl.ds(t * tile, tile)
            product = lax.dot_general(
                cen[at, :], vecs, (((1,), (1,)), ((), ())), preferred_element_type=F32
            )
            scores = 2.0 * product - norms[at, :]
            logit[slot, at, :] = scores
            high = jnp.max(scores, axis=0, keepdims=True)
            top = high if top is None else jnp.maximum(top, high)
        weight = None
        for t in range(tiles):
            at = pl.ds(t * tile, tile)
            p = jnp.exp(logit[slot, at, :] - top)
            prob[at, :] = p.astype(BF16)
            low = jnp.sum(p, axis=0, keepdims=True)
            weight = low if weight is None else weight + low
        first = lax.broadcasted_iota(jnp.int32, (8, rows), 0) < 4
        stats[far, n + nn * far, k] = jnp.where(first, top, weight)
        return far, k, slot, jnp.dot(cen_t[...], prob[...], preferred_element_type=F32)

    def m_copy(step):
        far = step // nn
        k = lax.rem(n + step, nn)
        slot = n + nn * far
        return remote(
            parts.at[step], got.at[slot], m_send.at[step], m_recv.at[slot],
            lax.rem(b + far, nb), k,
        )

    def s_copies(far):
        me = n + nn * far
        copies = []
        for j in range(nn):
            other = lax.rem(n + j, nn)
            if far:
                targets = [(after, 0, n + nn)] + ([(b, 1, n + nn)] if j else [])
            else:
                targets = ([(b, 0, n)] if j else []) + [(before, 1, n)]
            for i, (blk, group, where) in enumerate(targets):
                at = 2 * j + i
                copies.append(remote(
                    stats.at[far, me], stats.at[group, where], s_send.at[far, at],
                    s_recv.at[group, where], blk, other,
                ))
        return copies

    def attend_and_send(step):
        slot = lax.rem(n + step, nn) + nn * (step // nn)
        remote(
            vec_ref, v_all.at[slot], v_send.at[0], v_recv.at[slot], before, n
        ).wait_recv()
        mixed = attend(step)[3]
        parts[step] = mixed.astype(BF16)
        m_copy(step).start()

    mine[...] = attend(0)[3]

    @pl.loop(1, nn)
    def _(step):
        attend_and_send(step)

    for copy in s_copies(0):
        copy.start()

    @pl.loop(nn, 2 * nn)
    def _(step):
        attend_and_send(step)

    for copy in s_copies(1):
        copy.start()

    for group in range(2):
        me = n + nn * group

        @pl.loop(1, 2 * nn)
        def _(i, group=group, me=me):
            where = lax.rem(me + i, 2 * nn)
            remote(
                stats.at[group, where], stats.at[group, where], s_send.at[0, 0],
                s_recv.at[group, where], before, n,
            ).wait_recv()

    for group in range(2):
        for k in range(nn):
            tops = [stats[group, i, k][0:1, :] for i in range(2 * nn)]
            lows = [stats[group, i, k][4:5, :] for i in range(2 * nn)]
            top = functools.reduce(jnp.maximum, tops)
            mass = sum(low * jnp.exp(t - top) for t, low in zip(tops, lows))
            total[group * nn + k] = jnp.broadcast_to(top + jnp.log(mass), (8, rows))

    step_rows = cents // 8

    def o_copy(t):
        at = pl.ds(pl.multiple_of(t * step_rows, 16), step_rows)
        return pltpu.make_async_copy(acc.at[at], sums_ref.at[at], o_sem.at[t])

    def sum_up(t):
        at = pl.ds(pl.multiple_of(t * step_rows, 16), step_rows)
        weights = jnp.concatenate(
            [jnp.exp(logit[k, at, :] - total[k][0:1, :]).astype(BF16) for k in range(2 * nn)],
            axis=1,
        )
        acc[at, :] = jnp.dot(
            weights, v_all[...].reshape(2 * nn * rows, width), preferred_element_type=F32
        )
        tally = lax.dot_general(
            jnp.ones((8, 2 * nn * rows), BF16), weights, (((1,), (1,)), ((), ())),
            preferred_element_type=F32,
        )
        counts_ref[pl.ds(t, 1)] = tally[None, 0:1, :]
        o_copy(t).start()

    @pl.loop(0, EARLY)
    def _(t):
        sum_up(t)

    own_total = total[n][0:1, :]
    mine[...] = mine[...] * jnp.exp(stats[0, n, n][0:1, :] - own_total)

    @pl.loop(1, 2 * nn)
    def _(i):
        where = lax.rem(n + i, 2 * nn)
        remote(
            got.at[where], got.at[where], m_send.at[0], m_recv.at[where], before, n
        ).wait_recv()
        mine[...] += got[where].astype(F32) * jnp.exp(stats[0, where, n][0:1, :] - own_total)

    residual = (vec_t[...].astype(F32) - mine[...]).astype(BF16)
    box[...] = lax.dot_general(
        place[...], residual, (((1,), (1,)), ((), ())), preferred_element_type=F32
    ).astype(BF16)

    def block_of(i):
        return pl.ds(pl.multiple_of(i * cap, 16), cap)

    def a_copy(i):
        to = lax.rem(b + i, nb)
        return remote(
            box.at[block_of(to)], posted_ref.at[block_of(b)], a_send.at[i], a_recv.at[b], to, n
        )

    @pl.loop(1, nb)
    def _(i):
        a_copy(i).start()

    kept = pltpu.make_async_copy(
        box.at[block_of(b)], posted_ref.at[block_of(b)], local_sem.at[2]
    )
    kept.start()

    @pl.loop(EARLY, 8)
    def _(t):
        sum_up(t)

    @pl.loop(0, 8)
    def _(t):
        o_copy(t).wait()

    kept.wait()
    for j in range(nn):
        v_copy(j, 1).wait_send()
        if j:
            v_copy(j, 0).wait_send()
    for far in range(2):
        for copy in s_copies(far):
            copy.wait_send()

    @pl.loop(1, 2 * nn)
    def _(step):
        m_copy(step).wait_send()

    @pl.loop(1, nb)
    def _(i):
        source = lax.rem(b + i, nb)
        a_copy(i).wait_send()
        remote(
            box.at[block_of(source)], posted_ref.at[block_of(source)], a_send.at[i],
            a_recv.at[source], source, n,
        ).wait_recv()


def body(vectors, centroids, list_owner, list_local):
    nb, nn = lax.axis_size("blk"), lax.axis_size("narrow")
    rows, width = vectors.shape
    cents = centroids.shape[0] // nn
    cap = max(2, 2 * rows // nb)
    vmem = pl.BlockSpec(memory_space=pltpu.VMEM)
    hbm = pl.BlockSpec(memory_space=pl.ANY)
    dma = pltpu.SemaphoreType.DMA
    sums, counts, posted = pl.pallas_call(
        functools.partial(kernel, nb, nn, cap),
        out_shape=(
            jax.ShapeDtypeStruct((cents, width), F32),
            jax.ShapeDtypeStruct((8, 1, cents // 8), F32),
            jax.ShapeDtypeStruct((nb * cap, width), BF16),
        ),
        in_specs=[hbm, hbm, vmem, vmem],
        out_specs=(hbm, vmem, hbm),
        scratch_shapes=[
            pltpu.VMEM((2 * nn, rows, width), BF16),
            pltpu.VMEM((cents, width), BF16),
            pltpu.VMEM((width, cents), BF16),
            pltpu.VMEM((width, rows), BF16),
            pltpu.VMEM((cents, 1), F32),
            pltpu.VMEM((2 * nn, cents, rows), F32),
            pltpu.VMEM((cents, rows), BF16),
            pltpu.VMEM((2, 2 * nn, nn, 8, rows), F32),
            pltpu.VMEM((width, rows), F32),
            pltpu.VMEM((2 * nn, width, rows), BF16),
            pltpu.VMEM((2 * nn, width, rows), BF16),
            pltpu.VMEM((2 * nn, 8, rows), F32),
            pltpu.VMEM((nb * cap, rows), BF16),
            pltpu.VMEM((nb * cap, width), BF16),
            pltpu.VMEM((cents, width), F32),
            dma((3,)),
            dma((2 * nn,)),
            dma((2 * nn,)),
            dma((2, 2 * nn)),
            dma((2, 2 * nn)),
            dma((2 * nn,)),
            dma((2 * nn,)),
            dma((nb,)),
            dma((nb,)),
            dma((8,)),
        ],
        compiler_params=pltpu.CompilerParams(
            collective_id=0, has_side_effects=True, vmem_limit_bytes=56 * 1024 * 1024
        ),
        cost_estimate=pl.CostEstimate(
            flops=6 * 2 * nn * rows * cents * width, bytes_accessed=20 * cents * width,
            transcendentals=4 * nn * rows * cents,
        ),
    )(vectors, centroids, list_owner, list_local.reshape(1, rows))
    return sums, counts.reshape(cents), posted


def solution(mesh):
    in_specs = (
        P(("blk", "narrow"), None),
        P("blk", None),
        P(("blk", "narrow"), None),
        P(("blk", "narrow")),
    )
    out_specs = (P(("blk", "narrow"), None), P(("blk", "narrow")), P(("blk", "narrow"), None))
    return jax.shard_map(body, mesh=mesh, in_specs=in_specs, out_specs=out_specs, check_vma=False)
```

time: 348 us -> 78.5 us (0.23)
  waiting for transfers between devices: 222 us -> 0 us
  Pallas kernels: 0 us -> 68.7 us
  local copies, waits for them, and re-layouts: 45.9 us -> 8.93 us
  other arithmetic: 30.4 us -> 0 us
  matrix products: 23.9 us -> 0 us
  between operations: 14.2 us -> 0.66 us
  starting transfers between devices: 8.88 us -> 0 us
    ppermute x3 -> x0, waiting for transfers between devices: 128 us -> none  [passed_along(): return lax.ppermute(x, axis, [(i, (i + by) % peers) for i in range(peers)])]
    reduce_scatter x1 -> x0, waiting for transfers between devices: 76.4 us -> none  [body(): lax.psum_scatter(jnp.stack([pair[0] for pair in home_terms]), 'narrow', s...]
    pallas_call x0 -> x1, Pallas kernels: none -> 68.7 us  [body(): pl.pallas_call(functools.partial(kernel, nb, nn, cap), out_shape=(jax.Sha...]
    scatter x1 -> x0, local copies, waits for them, and re-layouts: 37.4 us -> none  [post_rows(): return buffer.at[sorted_owner, slot_index].set(residual[order])]
    dot_general x6 -> x0, matrix products: 23.9 us -> none  [the longest x2 9.83 us: body(): jnp.dot(weights, panel_rows, preferred_element_type=jnp.float32)]
    all_to_all x1 -> x0, waiting for transfers between devices: 17.7 us -> none  [body(): lax.all_to_all(buffer, 'blk', split_axis=0, concat_axis=0, tiled=True)]
    reduce_sum x8 -> x0, other arithmetic: 16 us -> none  [the longest x1 7.1 us: body(): panel_sums = jnp.sum(summed[0], axis=0)]
    another operation x4 -> x0, other arithmetic: 11.1 us -> none  [the longest x1 10.9 us: body(): jnp.stack([pair[0] for pair in home_terms])]
  transfers between devices with their start and end apart: 6 -> 0, of which waited for: 4 -> 0; matrix products, arithmetic and copies ran while one was open for 23% -> 0% of each run, Pallas kernels for 0% -> 0%
where the time goes in v1:
time: 78.5 us; the launch traced here: 78.3 us
  Pallas kernels  68.7 us (88%)
  local copies, waits for them, and re-layouts  8.93 us (11%)
    pallas_call x1, Pallas kernels, body(): pl.pallas_call(functools.partial(kernel, nb, nn, cap), out_shape=(jax.Sha...  68.7 us
    unnamed x8, local copies, waits for them, and re-layouts  8.93 us

profile of v1, /device:TPU:13, one launch (start us, length us, event | category | flops | bytes accessed | tf_op | source)
XLA Modules:
  0.0 78.3 jit_solution(3531033290353476277)
XLA Ops:
  0.6 1.5 %copy.7.owner_ref = s32[256,1]{1,0:T(8,128)} copy(s32[256,1]{0,1:T(1,128)} %param.6) | data formatting | bytes 2048 | tf_op args[2]
  2.1 68.7 %shard_map.67 = (f32[2048,768]{1,0:T(8,128)}, f32[8,1,256]{2,1,0:T(1,128)}, bf16[512,768]{1,0:T(8,128)(2,1)}) custom-call(bf16[256,768]{1,0:T(8,128)(2,1)} %vec_ref.1, bf16[4096,768]{1,0:T(8,128)(2,1)} %cen_ref.1, s32[256,1]{1,0:T(8,128)} %copy.7.owner_ref, s32[1,256]{1,0:T(1,128)} %bitcast.3), custom_call_target="tpu_custom_call" | custom-call | flops 9663676416 | bytes 31457280 | tf_op jit(solution)/shard_map/pallas_call | solution.py:294
  70.9 0.0 copy-start.1
  70.9 0.0 copy-start
  70.9 6.0 %copy.11 = f32[2048,768]{1,0:T(8,128)} copy(f32[2048,768]{1,0:T(8,128)} %get-tuple-element.12) | data formatting | bytes 12582912
  76.8 0.0 copy-done.1
  76.8 0.6 copy.12
  77.4 0.0 copy-done
  77.4 0.9 %copy.13 = bf16[512,768]{1,0:T(8,128)(2,1)} copy(bf16[512,768]{1,0:T(8,128)(2,1)S(1)} %copy-done) | data formatting | bytes 1572864
Async XLA Ops:
  70.9 6.0 %copy-start.1 = (f32[8,1,256]{2,1,0:T(1,128)S(1)}, f32[8,1,256]{2,1,0:T(1,128)}, u32[]{:S(2)}) copy-start(f32[8,1,256]{2,1,0:T(1,128)} %get-tuple-element.7) | copy-start | bytes 24580
  70.9 6.6 %copy-start = (bf16[512,768]{1,0:T(8,128)(2,1)S(1)}, bf16[512,768]{1,0:T(8,128)(2,1)}, u32[]{:S(2)}) copy-start(bf16[512,768]{1,0:T(8,128)(2,1)} %get-tuple-element.14) | copy-start | bytes 2359300

commit v2 on v1

--- a/solution.py
+++ b/solution.py
@@ -10,7 +10,7 @@
 MESH = pl.DeviceIdType.MESH
 F32 = jnp.float32
 BF16 = jnp.bfloat16
-EARLY = 2
+PIECES = 2
 
 
 def kernel(
@@ -59,18 +59,21 @@
 
     pl.semaphore_wait(barrier, 3 * (nn - 1) + nb - 1)
 
-    def v_copy(j, back):
-        other = lax.rem(n + j, nn)
-        slot = n + nn * back
-        at = j + nn * back
+    def near_copy(j):
         return remote(
-            vec_ref, v_all.at[slot], v_send.at[at], v_recv.at[slot], before if back else b, other
-        )
-
-    for j in range(nn):
-        v_copy(j, 1).start()
-        if j:
-            v_copy(j, 0).start()
+            vec_ref, v_all.at[n], v_send.at[j], v_recv.at[n], b, lax.rem(n + j, nn)
+        )
+
+    def far_copy(step):
+        k = lax.rem(n + step, nn)
+        source = vec_ref if isinstance(step, int) else v_all.at[k]
+        return remote(
+            source, v_all.at[nn + k], v_send.at[nn + step], v_recv.at[nn + k], before, n
+        )
+
+    for j in range(1, nn):
+        near_copy(j).start()
+    far_copy(0).start()
 
     own_cents.wait()
     for t in range(tiles):
@@ -84,9 +87,9 @@
 
     up = lax.broadcasted_iota(jnp.int32, (rows, rows), 0)
     across = lax.broadcasted_iota(jnp.int32, (rows, rows), 1)
-    owner_col = owner_ref[...].astype(F32)
+    owner_row = owner_ref[...].astype(F32)
     local_row = local_ref[...].astype(F32)
-    owner_row = jnp.sum(jnp.where(up == across, owner_col, 0.0), axis=0, keepdims=True)
+    owner_col = jnp.sum(jnp.where(up == across, owner_row, 0.0), axis=1, keepdims=True)
     local_col = jnp.sum(jnp.where(up == across, local_row, 0.0), axis=1, keepdims=True)
     ahead = (local_col < local_row) | ((local_col == local_row) & (up < across))
     rank = jnp.sum(
@@ -122,13 +125,16 @@
         stats[far, n + nn * far, k] = jnp.where(first, top, weight)
         return far, k, slot, jnp.dot(cen_t[...], prob[...], preferred_element_type=F32)
 
-    def m_copy(step):
+    part = width // PIECES
+
+    def m_copy(step, piece):
         far = step // nn
         k = lax.rem(n + step, nn)
         slot = n + nn * far
+        at = pl.ds(piece * part, part)
         return remote(
-            parts.at[step], got.at[slot], m_send.at[step], m_recv.at[slot],
-            lax.rem(b + far, nb), k,
+            parts.at[step, at], got.at[slot, at], m_send.at[piece, step],
+            m_recv.at[piece, slot], lax.rem(b + far, nb), k,
         )
 
     def s_copies(far):
@@ -148,30 +154,38 @@
                 ))
         return copies
 
-    def attend_and_send(step):
+    def wait_rows(step):
         slot = lax.rem(n + step, nn) + nn * (step // nn)
         remote(
             vec_ref, v_all.at[slot], v_send.at[0], v_recv.at[slot], before, n
         ).wait_recv()
-        mixed = attend(step)[3]
-        parts[step] = mixed.astype(BF16)
-        m_copy(step).start()
 
     mine[...] = attend(0)[3]
 
     @pl.loop(1, nn)
     def _(step):
-        attend_and_send(step)
+        wait_rows(step)
+        far_copy(step).start()
+        parts[step] = attend(step)[3].astype(BF16)
+        for piece in range(PIECES):
+            m_copy(step, piece).start()
 
     for copy in s_copies(0):
         copy.start()
 
     @pl.loop(nn, 2 * nn)
     def _(step):
-        attend_and_send(step)
+        wait_rows(step)
+        parts[step] = attend(step)[3].astype(BF16)
+        m_copy(step, 0).start()
 
     for copy in s_copies(1):
         copy.start()
+
+    @pl.loop(nn, 2 * nn)
+    def _(step):
+        for piece in range(1, PIECES):
+            m_copy(step, piece).start()
 
     for group in range(2):
         me = n + nn * group
@@ -214,45 +228,48 @@
         counts_ref[pl.ds(t, 1)] = tally[None, 0:1, :]
         o_copy(t).start()
 
-    @pl.loop(0, EARLY)
-    def _(t):
-        sum_up(t)
-
-    own_total = total[n][0:1, :]
-    mine[...] = mine[...] * jnp.exp(stats[0, n, n][0:1, :] - own_total)
-
-    @pl.loop(1, 2 * nn)
-    def _(i):
-        where = lax.rem(n + i, 2 * nn)
-        remote(
-            got.at[where], got.at[where], m_send.at[0], m_recv.at[where], before, n
-        ).wait_recv()
-        mine[...] += got[where].astype(F32) * jnp.exp(stats[0, where, n][0:1, :] - own_total)
-
-    residual = (vec_t[...].astype(F32) - mine[...]).astype(BF16)
-    box[...] = lax.dot_general(
-        place[...], residual, (((1,), (1,)), ((), ())), preferred_element_type=F32
-    ).astype(BF16)
-
     def block_of(i):
         return pl.ds(pl.multiple_of(i * cap, 16), cap)
 
-    def a_copy(i):
+    def a_copy(i, piece):
         to = lax.rem(b + i, nb)
+        at = pl.ds(piece * part, part)
         return remote(
-            box.at[block_of(to)], posted_ref.at[block_of(b)], a_send.at[i], a_recv.at[b], to, n
-        )
-
-    @pl.loop(1, nb)
-    def _(i):
-        a_copy(i).start()
+            box.at[block_of(to), at], posted_ref.at[block_of(b), at], a_send.at[piece, i],
+            a_recv.at[piece, b], to, n,
+        )
+
+    own_total = total[n][0:1, :]
+    own_share = jnp.exp(stats[0, n, n][0:1, :] - own_total)
+    for piece in range(PIECES):
+        at = pl.ds(piece * part, part)
+        mine[at, :] = mine[at, :] * own_share
+
+        @pl.loop(1, 2 * nn)
+        def _(i, piece=piece, at=at):
+            where = lax.rem(n + i, 2 * nn)
+            remote(
+                got.at[where, at], got.at[where, at], m_send.at[0, 0],
+                m_recv.at[piece, where], before, n,
+            ).wait_recv()
+            share = jnp.exp(stats[0, where, n][0:1, :] - own_total)
+            mine[at, :] += got[where, at, :].astype(F32) * share
+
+        residual = (vec_t[at, :].astype(F32) - mine[at, :]).astype(BF16)
+        box[:, at] = lax.dot_general(
+            place[...], residual, (((1,), (1,)), ((), ())), preferred_element_type=F32
+        ).astype(BF16)
+
+        @pl.loop(1, nb)
+        def _(i, piece=piece):
+            a_copy(i, piece).start()
 
     kept = pltpu.make_async_copy(
         box.at[block_of(b)], posted_ref.at[block_of(b)], local_sem.at[2]
     )
     kept.start()
 
-    @pl.loop(EARLY, 8)
+    @pl.loop(0, 8)
     def _(t):
         sum_up(t)
 
@@ -261,26 +278,31 @@
         o_copy(t).wait()
 
     kept.wait()
-    for j in range(nn):
-        v_copy(j, 1).wait_send()
-        if j:
-            v_copy(j, 0).wait_send()
+    far_copy(0).wait_send()
     for far in range(2):
         for copy in s_copies(far):
             copy.wait_send()
 
-    @pl.loop(1, 2 * nn)
+    @pl.loop(1, nn)
     def _(step):
-        m_copy(step).wait_send()
-
-    @pl.loop(1, nb)
-    def _(i):
-        source = lax.rem(b + i, nb)
-        a_copy(i).wait_send()
-        remote(
-            box.at[block_of(source)], posted_ref.at[block_of(source)], a_send.at[i],
-            a_recv.at[source], source, n,
-        ).wait_recv()
+        near_copy(step).wait_send()
+        far_copy(step).wait_send()
+
+    for piece in range(PIECES):
+        at = pl.ds(piece * part, part)
+
+        @pl.loop(1, 2 * nn)
+        def _(step, piece=piece):
+            m_copy(step, piece).wait_send()
+
+        @pl.loop(1, nb)
+        def _(i, piece=piece, at=at):
+            source = lax.rem(b + i, nb)
+            a_copy(i, piece).wait_send()
+            remote(
+                box.at[block_of(source), at], posted_ref.at[block_of(source), at],
+                a_send.at[piece, i], a_recv.at[piece, source], source, n,
+            ).wait_recv()
 
 
 def body(vectors, centroids, list_owner, list_local):
@@ -321,10 +343,10 @@
             dma((2 * nn,)),
             dma((2, 2 * nn)),
             dma((2, 2 * nn)),
-            dma((2 * nn,)),
-            dma((2 * nn,)),
-            dma((nb,)),
-            dma((nb,)),
+            dma((PIECES, 2 * nn)),
+            dma((PIECES, 2 * nn)),
+            dma((PIECES, nb)),
+            dma((PIECES, nb)),
             dma((8,)),
         ],
         compiler_params=pltpu.CompilerParams(
@@ -334,7 +356,7 @@
             flops=6 * 2 * nn * rows * cents * width, bytes_accessed=20 * cents * width,
             transcendentals=4 * nn * rows * cents,
         ),
-    )(vectors, centroids, list_owner, list_local.reshape(1, rows))
+    )(vectors, centroids, list_owner.reshape(1, rows), list_local.reshape(1, rows))
     return sums, counts.reshape(cents), posted
 
 

time: 78.5 us -> 65.4 us (0.83)
  Pallas kernels: 68.7 us -> 57 us
  local copies, waits for them, and re-layouts: 8.93 us -> 7.45 us
    pallas_call x1, Pallas kernels: 68.7 us -> 57 us  [body(): pl.pallas_call(functools.partial(kernel, nb, nn, cap), out_shape=(jax.Sha...]
    unnamed x8 -> x7, local copies, waits for them, and re-layouts: 8.93 us -> 7.45 us
where the time goes in v2:
time: 65.4 us; the launch traced here: 65.1 us
  Pallas kernels  57 us (87%)
  local copies, waits for them, and re-layouts  7.45 us (11%)
  between operations  0.66 us (1%)
    pallas_call x1, Pallas kernels, body(): pl.pallas_call(functools.partial(kernel, nb, nn, cap), out_shape=(jax.Sha...  57 us
    unnamed x7, local copies, waits for them, and re-layouts  7.45 us

profile of v2, /device:TPU:13, one launch (start us, length us, event | category | flops | bytes accessed | tf_op | source)
XLA Modules:
  0.0 65.1 jit_solution(6664492453637501968)
XLA Ops:
  0.6 57.0 %shard_map.67 = (f32[2048,768]{1,0:T(8,128)}, f32[8,1,256]{2,1,0:T(1,128)}, bf16[512,768]{1,0:T(8,128)(2,1)}) custom-call(bf16[256,768]{1,0:T(8,128)(2,1)} %vec_ref.1, bf16[4096,768]{1,0:T(8,128)(2,1)} %cen_ref.1, s32[1,256]{1,0:T(1,128)} %bitcast.4, s32[1,256]{1,0:T(1,128)} %bitcast.5), custom_call_target="tpu_custom_call" | custom-call | flops 9663676416 | bytes 31457280 | tf_op jit(solution)/shard_map/pallas_call | solution.py:316
  57.6 0.0 copy-start.1
  57.6 0.0 copy-start
  57.6 6.0 %copy.10 = f32[2048,768]{1,0:T(8,128)} copy(f32[2048,768]{1,0:T(8,128)} %get-tuple-element.12) | data formatting | bytes 12582912
  63.6 0.0 copy-done.1
  63.6 0.6 copy.11
  64.2 0.0 copy-done
  64.2 0.9 %copy.12 = bf16[512,768]{1,0:T(8,128)(2,1)} copy(bf16[512,768]{1,0:T(8,128)(2,1)S(1)} %copy-done) | data formatting | bytes 1572864
Async XLA Ops:
  57.6 6.0 %copy-start.1 = (f32[8,1,256]{2,1,0:T(1,128)S(1)}, f32[8,1,256]{2,1,0:T(1,128)}, u32[]{:S(2)}) copy-start(f32[8,1,256]{2,1,0:T(1,128)} %get-tuple-element.7) | copy-start | bytes 24580
  57.6 6.6 %copy-start = (bf16[512,768]{1,0:T(8,128)(2,1)S(1)}, bf16[512,768]{1,0:T(8,128)(2,1)}, u32[]{:S(2)}) copy-start(bf16[512,768]{1,0:T(8,128)(2,1)} %get-tuple-element.14) | copy-start | bytes 2359300
